TPU v7x, 512 devices: a whole 4x8x8 slice. The times are simulated.
512 devices in a mesh: rows: 128 (over z, y, core), cols: 4 (over x).
Axes of the slice: x: 4, y: 8, z: 8, core: 2. Of those that a mesh axis runs over, the one named last changes fastest.
Arguments:
- basis_cols: bfloat16 [524288, 1024], P('rows', 'cols'), may hold values from -6 to 6, as said below
- snapshots: bfloat16 [256, 524288], P(None, 'rows'), may hold values from -600 to 600
Outputs:
- coefficients: float32 [1024, 256], P('cols')
- factor: float32 [256, 256], replicated
- directions: bfloat16 [256, 524288], P(None, ('rows', 'cols'))
Inputs may be any that keep to these rules, and one draw needn't show every extreme that they name: `basis_cols`: normal entries.
All inputs are finite; a program needn't handle non-finite values.
Results may differ from a plain program's by a relative error of at most 0.0056.
Values may be sent and summed in bfloat16 or wider, within the bound.
A program may use at most 64 MiB of HBM per device.

v0:
```python
import math

import jax
import jax.numpy as jnp
from jax import lax
from jax.sharding import PartitionSpec as P

RANK = 1024


def shards(basis_cols, snapshots):
    col_count = lax.axis_size("cols")
    column_index = lax.axis_index("cols")
    total_points = snapshots.shape[1] * lax.axis_size("rows")
    part_rows = snapshots.shape[1] // col_count
    own_snaps = lax.dynamic_slice_in_dim(snapshots, column_index * part_rows, part_rows, 1)
    coeff_scale = math.sqrt(RANK) / total_points
    partial_value = lax.dot_general(
        basis_cols, snapshots, (((0,), (1,)), ((), ())), preferred_element_type=jnp.float32
    )
    coefficients = lax.psum(partial_value, "rows") * coeff_scale
    coeff_low = coefficients.astype(jnp.bfloat16)
    recon_part = lax.dot_general(
        coeff_low, basis_cols, (((0,), (1,)), ((), ())), preferred_element_type=jnp.float32
    )
    recon = lax.psum_scatter(recon_part, "cols", scatter_dimension=1, tiled=True) / math.sqrt(RANK)
    residual = own_snaps.astype(jnp.float32) - recon
    partial_gram = jnp.dot(residual, residual.T, precision=lax.Precision.HIGHEST) / total_points
    gram = lax.psum(partial_gram, ("rows", "cols"))
    factor = jnp.linalg.cholesky(gram)
    directions = lax.linalg.triangular_solve(factor, residual, left_side=True, lower=True).astype(
        jnp.bfloat16
    )
    return (coefficients, factor, directions)


def solution(mesh):
    placed = (P("rows", "cols"), P(None, "rows"))
    return jax.shard_map(
        shards,
        mesh=mesh,
        in_specs=placed,
        out_specs=(P("cols", None), P(), P(None, ("rows", "cols"))),
        check_vma=False,
    )
```

profile of v0, /device:TPU:1, one launch (start us, length us, event | category | flops | bytes accessed | tf_op | source)
XLA Modules:
  0.0 610.5 jit_solution(12687404624838463654)
XLA Ops:
  7.2 0.0 copy-start
  7.2 0.0 all-reduce.4.cloned.1.call-start
  7.2 1.5 copy-done
  8.8 3.0 fusion.12
  11.8 0.0 all-reduce.4.cloned.1.call-update
  11.8 0.0 reduce-scatter.2.cloned.1.call-start
  11.9 194.3 %all-reduce.4.cloned.1.call-done = f32[256,256]{1,0:T(8,128)} async-done(((f32[256,256]{1,0:T(8,128)}), f32[256,256]{1,0:T(8,128)}) %all-reduce.4.cloned.1.call-update) | async-done | bytes 262160 | tf_op jit(solution)/shard_map/psum | solution.py:21
  206.2 1.0 broadcast_multiply_fusion
  207.2 0.0 copy-start.1
  207.2 2.7 fusion.4
  209.9 0.0 copy-done.1
  209.9 0.0 reduce-scatter.2.cloned.1.call-update
  209.9 0.0 all-reduce.6.cloned.1.call-start
  210.0 50.1 %reduce-scatter.2.cloned.1.call-done = f32[256,1024]{1,0:T(8,128)} async-done(((f32[256,4096]{1,0:T(8,128)}), f32[256,1024]{1,0:T(8,128)}) %reduce-scatter.2.cloned.1.call-update) | async-done | bytes 1048592 | tf_op jit(solution)/shard_map/reduce_scatter | solution.py:26
  260.1 1.5 multiply_subtract_fusion
  261.7 1.7 convolution_multiply_fusion
  263.4 0.0 all-reduce.6.cloned.1.call-update
  263.4 270.4 %all-reduce.6.cloned.1.call-done = f32[256,256]{0,1:T(8,128)} async-done(((f32[256,256]{0,1:T(8,128)}), f32[256,256]{0,1:T(8,128)}) %all-reduce.6.cloned.1.call-update) | async-done | bytes 262160 | tf_op jit(solution)/shard_map/psum | solution.py:29
  533.8 1.1 copy.6
  534.9 1.0 fusion.2
  535.9 0.0 copy-start.3
  535.9 0.7 copy-done.3
  536.6 11.7 %cholesky.50 = f32[128,128]{1,0:T(8,128)S(1)} custom-call(f32[128,128]{1,0:T(8,128)S(1)} %cholesky.118), custom_call_target="Cholesky" | custom-call | tf_op jit(solution)/shard_map/jit(cholesky)/cholesky | solution.py:30
  548.4 9.8 %custom-call.14 = f32[1,128,128]{1,2,0:T(8,128)S(1)} custom-call(f32[1,128,128]{2,1,0:T(8,128)S(1)} %get-tuple-element.26), custom_call_target="InvertDiagBlocksLowerTriangular" | custom-call | tf_op jit(solution)/shard_map/jit(cholesky)/cholesky | solution.py:30
  558.2 1.0 constant_dynamic-update-slice_fusion.1
  559.3 1.1 convolution_subtract_fusion.1
  560.4 11.7 %cholesky.105 = f32[128,128]{1,0:T(8,128)S(1)} custom-call(f32[128,128]{1,0:T(8,128)S(1)} %convolution_subtract_fusion.1), custom_call_target="Cholesky" | custom-call | tf_op jit(solution)/shard_map/jit(cholesky)/cholesky | solution.py:30
  572.1 0.0 copy-start.2
  572.1 0.7 compare_reduce_fusion
  574.0 0.0 copy-done.2
  574.0 1.7 fusion.3
  575.7 0.1 triangular_solve.42
  575.8 5.0 while.1
  575.8 0.6 fusion.23
  576.4 1.9 bitcast_dynamic-update-slice_fusion.2
  578.3 0.6 fusion.23
  578.9 1.9 bitcast_dynamic-update-slice_fusion.2
  580.8 20.5 %custom-call.15 = f32[2,128,128]{1,2,0:T(8,128)S(1)} custom-call(f32[2,128,128]{2,1,0:T(8,128)} %get-tuple-element.10), custom_call_target="InvertDiagBlocksLowerTriangular" | custom-call | tf_op jit(solution)/shard_map/triangular_solve | solution.py:31
  601.3 0.6 fusion.11
  601.9 0.6 convolution_subtract_fusion
  602.5 0.6 convolution_convert_fusion
  603.1 0.8 pad_maximum_fusion
  (8 shorter events, 0.1 us)
Async XLA Ops:
  7.2 1.6 copy-start
  7.2 199.0 %all-reduce.4.cloned.1.call-start = ((), (), s32[]{:S(2)}) async-start(), calls=%async_computation.1 | async-start | bytes 524288 | tf_op jit(solution)/shard_map/psum | solution.py:21
  11.8 248.3 %reduce-scatter.2.cloned.1.call-start = ((), (), s32[]{:S(2)}) async-start(), calls=%async_computation.2 | async-start | bytes 5242880 | tf_op jit(solution)/shard_map/reduce_scatter | solution.py:26
  207.2 2.7 copy-start.1
  209.9 323.9 %all-reduce.6.cloned.1.call-start = ((), (), s32[]{:S(2)}) async-start(), calls=%async_computation.3 | async-start | bytes 524288 | tf_op jit(solution)/shard_map/psum | solution.py:29
  535.9 0.7 copy-start.3
  572.1 1.9 copy-start.2
Sparse Core Ops, SparseCore 0:
  12.0 194.2 all-reduce.3
  210.1 50.0 reduce-scatter.1
  266.5 267.3 all-reduce.5
where the time goes:
time: 611 us; the launch traced here: 610 us
  waiting for transfers between devices  515 us (84%)
  other arithmetic  60.5 us (10%)
  between operations  15.1 us (2%)
  matrix products  11.5 us (2%)
  local copies, waits for them, and re-layouts  8.42 us (1%)
    psum x1, waiting for transfers between devices, shards(): gram = lax.psum(partial_gram, ('rows', 'cols'))  270 us
    psum x1, waiting for transfers between devices, shards(): coefficients = lax.psum(partial_value, 'rows') * coeff_scale  194 us
    reduce_scatter x1, waiting for transfers between devices, shards(): lax.psum_scatter(recon_part, 'cols', scatter_dimension=1, tiled=True)  50.1 us
    another operation x6, other arithmetic, shards(): factor = jnp.linalg.cholesky(gram)  34 us
    another operation x4, other arithmetic, shards(): lax.linalg.triangular_solve(factor, residual, left_side=True, lower=True)  23 us
  transfers between devices with their start and end apart: 3, of which 3 were waited for; matrix products, arithmetic and copies ran while one was open for 0% of the time, Pallas kernels for 0%

commit v1 on v0

v1 whole, which is shorter than its diff:
```python
import functools
import math

import jax
import jax.numpy as jnp
from jax import lax
from jax.experimental import pallas as pl
from jax.experimental.pallas import tpu as pltpu
from jax.sharding import PartitionSpec as P

RANK = 1024
SIDE_Y = 8
MESH = pl.DeviceIdType.MESH
F32 = jnp.float32
BF16 = jnp.bfloat16
HALF = 128


def exchange(kernel_kernel, b_hbm, s_hbm, coef_o, gram_o, res_o, bv, sv, bfull, qfull, cbuf,
             pbuf, gbuf, core_in, rs_in, ar_in, x_in, part, ag, load_sem, bx_s, bx_r, qx_s, qx_r,
             qc_s, qc_r, cc_s, cc_r, core_s, core_r, rs_s, rs_r, ar_s, ar_r, ag_s, ag_r, x_s, x_r,
             gc_s, gc_r):
    ny, nz, nx, points = kernel_kernel
    row, x = lax.axis_index("rows"), lax.axis_index("cols")
    z, y, c = row // (2 * ny), (row // 2) % ny, row % 2
    own_points = b_hbm.shape[0] // nx

    def device(z, y, c, x):
        return ((z * ny + y) * 2 + c, x)

    def ring(me, n):
        return [lax.rem(me + k, n) for k in range(1, n)]

    y_peers, z_peers, x_peers = ring(y, ny), ring(z, nz), ring(x, nx)
    mate = device(z, y, 1 - c, x)

    first = ((y, ny, y_peers, lambda t: device(z, t, c, x)), (z, nz, z_peers, lambda t: device(t, y, c, x)))
    second = (first[1], first[0])

    def remote(src, dst, send, recv, dev):
        return pltpu.make_async_remote_copy(
            src_ref=src, dst_ref=dst, send_sem=send, recv_sem=recv, device_id=dev, device_id_type=MESH
        )

    load_b = pltpu.make_async_copy(b_hbm, bv, load_sem.at[0])
    load_s = pltpu.make_async_copy(s_hbm, sv, load_sem.at[1])
    load_b.start()
    load_s.start()

    barrier = pltpu.get_barrier_semaphore()
    peers = [mate] + [device(z, t, c, x) for t in y_peers] + [device(t, y, c, x) for t in z_peers]
    peers += [device(z, y, c, t) for t in x_peers]
    for peer in peers:
        pl.semaphore_signal(barrier, inc=1, device_id=peer, device_id_type=MESH)
    pl.semaphore_wait(barrier, len(peers))

    pending = []

    for t in x_peers:
        copy = remote(b_hbm.at[pl.ds(t * own_points, own_points)], bfull.at[x], bx_s.at[t], bx_r.at[x],
                      device(z, y, c, t))
        copy.start()
        pending.append(copy)
    load_own = pltpu.make_async_copy(b_hbm.at[pl.ds(x * own_points, own_points)], bfull.at[x], load_sem.at[2])
    load_own.start()

    load_b.wait()
    load_s.wait()
    steps = 4
    depth = b_hbm.shape[0] // steps
    total = None
    for k in range(steps):
        piece = jnp.dot(sv[:, k * depth:(k + 1) * depth], bv[k * depth:(k + 1) * depth, :],
                        preferred_element_type=F32)
        total = piece if total is None else total + piece

    def reduce(phase, buf, value, over_x):
        for h in range(2):
            for l in range(2):
                buf[h, l] = value[h * HALF:(h + 1) * HALF, l * HALF:(l + 1) * HALF]
        copy = remote(buf.at[1 - c], core_in.at[phase], core_s.at[phase], core_r.at[phase], mate)
        copy.start()
        pending.append(copy)
        copy.wait_recv()
        for l in range(2):
            me, n, ring_peers, dev = first[l]
            rows = HALF // n
            mine = buf[c, l] + core_in[phase, l]
            part[phase, 0, l] = mine
            for t in ring_peers:
                copy = remote(part.at[phase, 0, l, pl.ds(t * rows, rows)], rs_in.at[phase, l, me],
                              rs_s.at[phase, l, t], rs_r.at[phase, l, me], dev(t))
                copy.start()
                pending.append(copy)
            rs_in[phase, l, me] = part[phase, 0, l, pl.ds(pl.multiple_of(me * rows, rows), rows), :]
        for l in range(2):
            me, n, ring_peers, dev = first[l]
            for t in ring_peers:
                remote(rs_in.at[phase, l, t], rs_in.at[phase, l, t], rs_s.at[phase, l, t], rs_r.at[phase, l, t],
                       mate).wait_recv()
            got = rs_in[phase, l, 0]
            for i in range(1, n):
                got = got + rs_in[phase, l, i]
            me, n, ring_peers, dev = second[l]
            ar_in[phase, l, me] = got
            for t in ring_peers:
                copy = remote(ar_in.at[phase, l, me], ar_in.at[phase, l, me], ar_s.at[phase, l, t],
                              ar_r.at[phase, l, me], dev(t))
                copy.start()
                pending.append(copy)
        for l in range(2):
            me, n, ring_peers, dev = second[l]
            for t in ring_peers:
                remote(ar_in.at[phase, l, t], ar_in.at[phase, l, t], ar_s.at[phase, l, t], ar_r.at[phase, l, t],
                       mate).wait_recv()
            got = ar_in[phase, l, 0]
            for i in range(1, n):
                got = got + ar_in[phase, l, i]
            if over_x:
                x_in[x, l] = got
                for t in x_peers:
                    copy = remote(x_in.at[x, l], x_in.at[x, l], x_s.at[l, t], x_r.at[l, x], device(z, y, c, t))
                    copy.start()
                    pending.append(copy)
            else:
                me, n, ring_peers, dev = first[l]
                rows = HALF // n
                own = pl.ds(pl.multiple_of(me * rows, rows), rows)
                ag[phase, l, own, :] = got
        if over_x:
            for l in range(2):
                for t in x_peers:
                    remote(x_in.at[t, l], x_in.at[t, l], x_s.at[l, t], x_r.at[l, t], mate).wait_recv()
                got = x_in[0, l]
                for i in range(1, nx):
                    got = got + x_in[i, l]
                me, n, ring_peers, dev = first[l]
                rows = HALF // n
                own = pl.ds(pl.multiple_of(me * rows, rows), rows)
                ag[phase, l, own, :] = got
        for l in range(2):
            me, n, ring_peers, dev = first[l]
            rows = HALF // n
            own = pl.ds(pl.multiple_of(me * rows, rows), rows)
            for t in ring_peers:
                copy = remote(ag.at[phase, l, own], ag.at[phase, l, own], ag_s.at[phase, l, t],
                              ag_r.at[phase, l, me], dev(t))
                copy.start()
                pending.append(copy)
        for l in range(2):
            me, n, ring_peers, dev = first[l]
            rows = HALF // n
            for t in ring_peers:
                theirs = ag.at[phase, l, pl.ds(t * rows, rows)]
                remote(theirs, theirs, ag_s.at[phase, l, t], ag_r.at[phase, l, t], mate).wait_recv()

    reduce(0, pbuf, total, False)

    scale = math.sqrt(RANK) / points
    own = jnp.concatenate([ag[0, 0], ag[0, 1]], axis=1) * scale
    qfull[x, c] = own.astype(BF16)
    for t in x_peers:
        copy = remote(qfull.at[x, c], qfull.at[x, c], qx_s.at[t], qx_r.at[x], device(z, y, c, t))
        copy.start()
        pending.append(copy)
    cbuf[c] = own

    def to_mate(t):
        copy = remote(qfull.at[t, c], qfull.at[t, c], qc_s.at[t], qc_r.at[t], mate)
        copy.start()
        pending.append(copy)

    to_mate(x)
    copy = remote(cbuf.at[c], cbuf.at[c], cc_s, cc_r, mate)
    copy.start()
    pending.append(copy)
    for t in x_peers:
        remote(qfull.at[t, c], qfull.at[t, c], qx_s.at[t], qx_r.at[t], mate).wait_recv()
        to_mate(t)
    for t in range(nx):
        remote(qfull.at[t, 1 - c], qfull.at[t, 1 - c], qc_s.at[t], qc_r.at[t], mate).wait_recv()

    load_own.wait()
    for t in x_peers:
        remote(bfull.at[t], bfull.at[t], bx_s.at[t], bx_r.at[t], mate).wait_recv()
    recon = None
    for t in range(nx):
        piece = lax.dot_general(qfull[t].reshape(2 * HALF, 2 * HALF), bfull[t], (((1,), (1,)), ((), ())),
                                preferred_element_type=F32)
        recon = piece if recon is None else recon + piece
    own_snaps = sv[:, pl.ds(pl.multiple_of(x * own_points, own_points), own_points)].astype(F32)
    residual = own_snaps - recon * (1.0 / math.sqrt(RANK))
    res_o[...] = residual
    gram = lax.dot_general(residual, residual, (((1,), (1,)), ((), ())), precision=lax.Precision.HIGHEST,
                           preferred_element_type=F32) * (1.0 / points)
    reduce(1, gbuf, gram, True)
    gc = remote(ag.at[1], gbuf.at[2], gc_s, gc_r, mate)
    gc.start()
    pending.append(gc)
    remote(cbuf.at[1 - c], cbuf.at[1 - c], cc_s, cc_r, mate).wait_recv()
    for h in range(2):
        coef_o[:, h * HALF:(h + 1) * HALF] = cbuf[h].T
    rows_own = pl.ds(pl.multiple_of(c * HALF, HALF), HALF)
    rows_mate = pl.ds(pl.multiple_of((1 - c) * HALF, HALF), HALF)
    gram_o[rows_own, :] = jnp.concatenate([ag[1, 0], ag[1, 1]], axis=1)
    gc.wait_recv()
    gram_o[rows_mate, :] = jnp.concatenate([gbuf[2, 0], gbuf[2, 1]], axis=1)
    for copy in pending:
        copy.wait_send()


def shards(sides, basis_cols, snapshots):
    ny, nz, nx, points = sides
    own_points = basis_cols.shape[0] // nx
    modes = basis_cols.shape[1]
    snaps = snapshots.shape[0]
    n = max(ny, nz)
    dma = pltpu.SemaphoreType.DMA
    chunk = HALF // n
    coefficients, gram, residual = pl.pallas_call(
        functools.partial(exchange, sides),
        out_shape=(
            jax.ShapeDtypeStruct((modes, snaps), F32),
            jax.ShapeDtypeStruct((snaps, snaps), F32),
            jax.ShapeDtypeStruct((snaps, own_points), F32),
        ),
        in_specs=[pl.BlockSpec(memory_space=pl.ANY)] * 2,
        out_specs=(pl.BlockSpec(memory_space=pltpu.VMEM),) * 3,
        scratch_shapes=[
            pltpu.VMEM(basis_cols.shape, BF16),
            pltpu.VMEM(snapshots.shape, BF16),
            pltpu.VMEM((nx, own_points, modes), BF16),
            pltpu.VMEM((nx, 2, HALF, modes), BF16),
            pltpu.VMEM((2, HALF, modes), F32),
            pltpu.VMEM((2, 2, HALF, HALF), F32),
            pltpu.VMEM((3, 2, HALF, HALF), F32),
            pltpu.VMEM((2, 2, HALF, HALF), F32),
            pltpu.VMEM((2, 2, n, chunk, HALF), F32),
            pltpu.VMEM((2, 2, n, chunk, HALF), F32),
            pltpu.VMEM((nx, 2, chunk, HALF), F32),
            pltpu.VMEM((2, 1, 2, HALF, HALF), F32),
            pltpu.VMEM((2, 2, HALF, HALF), F32),
            dma((3,)),
            dma((nx,)), dma((nx,)),
            dma((nx,)), dma((nx,)),
            dma((nx,)), dma((nx,)),
            dma(()), dma(()),
            dma((2,)), dma((2,)),
            dma((2, 2, n)), dma((2, 2, n)),
            dma((2, 2, n)), dma((2, 2, n)),
            dma((2, 2, n)), dma((2, 2, n)),
            dma((2, nx)), dma((2, nx)),
            dma(()), dma(()),
        ],
        compiler_params=pltpu.CompilerParams(
            collective_id=0, has_side_effects=True, vmem_limit_bytes=48 << 20
        ),
        name="exchange",
    )(basis_cols, snapshots)
    factor = jnp.linalg.cholesky(gram)
    directions = lax.linalg.triangular_solve(factor, residual, left_side=True, lower=True).astype(BF16)
    return (coefficients, factor, directions)


def solution(mesh):
    rows, cols = mesh.shape["rows"], mesh.shape["cols"]
    placed = (P("rows", "cols"), P(None, "rows"))

    def whole(basis_cols, snapshots):
        sides = (SIDE_Y, rows // (2 * SIDE_Y), cols, basis_cols.shape[0])
        return jax.shard_map(
            functools.partial(shards, sides),
            mesh=mesh,
            in_specs=placed,
            out_specs=(P("cols", None), P(), P(None, ("rows", "cols"))),
            check_vma=False,
        )(basis_cols, snapshots)

    return whole
```

time: 611 us -> 138 us (0.23)
  waiting for transfers between devices: 515 us -> 0 us
  Pallas kernels: 0 us -> 70.3 us
  between operations: 15.1 us -> 2.03 us
  matrix products: 11.5 us -> 2.32 us
    psum x2 -> x0, waiting for transfers between devices: 465 us -> none  [the longest x1 270 us: shards(): gram = lax.psum(partial_gram, ('rows', 'cols'))]
    pallas_call x0 -> x1, Pallas kernels: none -> 70.3 us  [shards(): pl.pallas_call(functools.partial(exchange, sides), out_shape=(jax.ShapeDt...]
    reduce_scatter x1 -> x0, waiting for transfers between devices: 50.1 us -> none  [shards(): lax.psum_scatter(recon_part, 'cols', scatter_dimension=1, tiled=True)]
    dot_general x3 -> x0, matrix products: 7.49 us -> none  [the longest x1 3.05 us: shards(): lax.dot_general(basis_cols, snapshots, (((0,), (1,)), ((), ())), preferre...]
  transfers between devices with their start and end apart: 3 -> 0, of which waited for: 3 -> 0; matrix products, arithmetic and copies ran while one was open for 0% -> 0% of each run, Pallas kernels for 0% -> 0%
where the time goes in v1:
time: 138 us
  Pallas kernels  70.3 us (51%)
  other arithmetic  55.4 us (40%)
  local copies, waits for them, and re-layouts  8.17 us (6%)
  matrix products  2.32 us (2%)
  between operations  2.03 us (1%)
    pallas_call x1, Pallas kernels, shards(): pl.pallas_call(functools.partial(exchange, sides), out_shape=(jax.ShapeDt...  70.3 us
    another operation x6, other arithmetic, shards(): factor = jnp.linalg.cholesky(gram)  34.1 us
    another operation x4, other arithmetic, shards(): lax.linalg.triangular_solve(factor, residual, left_side=True, lower=True)  21.2 us
    another operation x6, local copies, waits for them, and re-layouts  4.06 us
    unnamed x5, local copies, waits for them, and re-layouts  3.88 us

profile of v1, /device:TPU:1, one launch (start us, length us, event | category | flops | bytes accessed | tf_op | source)
XLA Modules:
  0.0 138.2 jit_solution(10658491615120011865)
XLA Ops:
  0.6 0.1 triangular_solve.42
  0.7 0.0 copy-start
  0.7 1.6 %copy-done = bf16[4096,256]{1,0:T(8,128)(2,1)S(1)} copy-done((bf16[4096,256]{1,0:T(8,128)(2,1)S(1)}, bf16[4096,256]{1,0:T(8,128)(2,1)}, u32[]{:S(2)}) %copy-start) | copy-done | bytes 2097176
  2.3 0.0 copy-start.1
  2.3 1.6 %copy-done.1 = bf16[256,4096]{1,0:T(8,128)(2,1)S(1)} copy-done((bf16[256,4096]{1,0:T(8,128)(2,1)S(1)}, bf16[256,4096]{1,0:T(8,128)(2,1)}, u32[]{:S(2)}) %copy-start.1) | copy-done | bytes 2097176
  3.9 70.3 %exchange.1 = (f32[256,256]{1,0:T(8,128)S(1)}, f32[256,256]{1,0:T(8,128)S(1)}, f32[256,1024]{1,0:T(8,128)S(1)}) custom-call(bf16[4096,256]{1,0:T(8,128)(2,1)S(1)} %copy-done, bf16[256,4096]{1,0:T(8,128)(2,1)S(1)} %copy-done.1), custom_call_target="tpu_custom_call" | custom-call | tf_op jit(solution)/shard_map/exchange/pallas_call | solution.py:220
  74.2 0.1 copy.5
  74.4 11.7 %cholesky.50 = f32[128,128]{1,0:T(8,128)S(1)} custom-call(f32[128,128]{1,0:T(8,128)S(1)} %cholesky.118), custom_call_target="Cholesky" | custom-call | tf_op jit(solution)/shard_map/jit(cholesky)/cholesky | solution.py:260
  86.1 9.8 %custom-call.14 = f32[1,128,128]{1,2,0:T(8,128)S(1)} custom-call(f32[1,128,128]{2,1,0:T(8,128)S(1)} %get-tuple-element.32), custom_call_target="InvertDiagBlocksLowerTriangular" | custom-call | tf_op jit(solution)/shard_map/jit(cholesky)/cholesky | solution.py:260
  95.9 0.2 constant_dynamic-update-slice_fusion.1
  96.2 0.3 convolution_subtract_fusion.1
  96.4 11.9 %cholesky.105 = f32[128,128]{1,0:T(8,128)S(1)} custom-call(f32[128,128]{1,0:T(8,128)S(1)} %convolution_subtract_fusion.1), custom_call_target="Cholesky" | custom-call | tf_op jit(solution)/shard_map/jit(cholesky)/cholesky | solution.py:260
  108.3 0.6 compare_reduce_fusion
  110.3 0.7 fusion.3
  111.0 4.1 %while.1 = (s32[]{:T(128)}, f32[256,256]{1,0:T(8,128)S(1)}, s32[2,2]{1,0:T(2,128)S(1)}, f32[2,128,128]{2,1,0:T(8,128)S(1)}, s32[]{:T(128)}) while((s32[]{:T(128)}, f32[256,256]{1,0:T(8,128)S(1)}, s32[2,2]{1,0:T(2,128)S(1)}, f32[2,128,128]{2,1,0:T(8,128)S(1)}, s32[]{:T(128)}) %tuple.29), condition=%wide.while_cond, body=%wide.while_body.sunk | while | flops 2 | bytes 131189 | solution.py:261
  111.0 0.6 fusion.15
  111.6 1.4 %bitcast_dynamic-update-slice_fusion.2 = f32[2,128,128]{2,1,0:T(8,128)S(1)} fusion(f32[2,128,128]{2,1,0:T(8,128)S(1)} %get-tuple-element.76, s32[]{:T(128)S(6)} %copy.11, f32[256,256]{1,0:T(8,128)S(1)} %get-tuple-element.79, s32[]{:T(128)} %bitcast.31, s32[]{:T(128)} %bitcast.32), kind=kLoop, calls=%fused_computation.clone.1 | loop fusion | bytes 131084 | tf_op jit(solution)/shard_map/triangular_solve
  113.1 0.6 fusion.15
  113.7 1.4 %bitcast_dynamic-update-slice_fusion.2 = f32[2,128,128]{2,1,0:T(8,128)S(1)} fusion(f32[2,128,128]{2,1,0:T(8,128)S(1)} %get-tuple-element.76, s32[]{:T(128)S(6)} %copy.11, f32[256,256]{1,0:T(8,128)S(1)} %get-tuple-element.79, s32[]{:T(128)} %bitcast.31, s32[]{:T(128)} %bitcast.32), kind=kLoop, calls=%fused_computation.clone.1 | loop fusion | bytes 131084 | tf_op jit(solution)/shard_map/triangular_solve
  115.1 19.7 %custom-call.15 = f32[2,128,128]{1,2,0:T(8,128)S(1)} custom-call(f32[2,128,128]{2,1,0:T(8,128)S(1)} %get-tuple-element.16), custom_call_target="InvertDiagBlocksLowerTriangular" | custom-call | tf_op jit(solution)/shard_map/triangular_solve | solution.py:261
  134.8 0.6 fusion.9
  135.4 0.6 convolution_subtract_fusion
  136.0 0.6 convolution_convert_fusion
  136.6 0.8 pad_maximum_fusion
  137.5 0.7 copy.18
  (9 shorter events, 0.2 us)
Async XLA Ops:
  0.7 1.6 %copy-start = (bf16[4096,256]{1,0:T(8,128)(2,1)S(1)}, bf16[4096,256]{1,0:T(8,128)(2,1)}, u32[]{:S(2)}) copy-start(bf16[4096,256]{1,0:T(8,128)(2,1)} %b_hbm.1) | copy-start | bytes 6291460
  2.3 1.6 %copy-start.1 = (bf16[256,4096]{1,0:T(8,128)(2,1)S(1)}, bf16[256,4096]{1,0:T(8,128)(2,1)}, u32[]{:S(2)}) copy-start(bf16[256,4096]{1,0:T(8,128)(2,1)} %s_hbm.1) | copy-start | bytes 6291460

commit v2 on v1

--- a/solution.py
+++ b/solution.py
@@ -16,11 +16,11 @@
 HALF = 128
 
 
-def exchange(kernel_kernel, b_hbm, s_hbm, coef_o, gram_o, res_o, bv, sv, bfull, qfull, cbuf,
+def exchange(sides, b_hbm, s_hbm, coef_o, gram_o, res_o, bv, sv, bfull, qfull, cbuf,
              pbuf, gbuf, core_in, rs_in, ar_in, x_in, part, ag, load_sem, bx_s, bx_r, qx_s, qx_r,
              qc_s, qc_r, cc_s, cc_r, core_s, core_r, rs_s, rs_r, ar_s, ar_r, ag_s, ag_r, x_s, x_r,
              gc_s, gc_r):
-    ny, nz, nx, points = kernel_kernel
+    ny, nz, nx, points = sides
     row, x = lax.axis_index("rows"), lax.axis_index("cols")
     z, y, c = row // (2 * ny), (row // 2) % ny, row % 2
     own_points = b_hbm.shape[0] // nx
@@ -209,6 +209,84 @@
         copy.wait_send()
 
 
+def eliminate(a, n):
+    lanes = 2 * n
+    count = n // 8
+    r_io = lax.broadcasted_iota(jnp.int32, (8, n), 0)
+    c_io = lax.broadcasted_iota(jnp.int32, (8, n), 1)
+    sub = lax.broadcasted_iota(jnp.int32, (8, lanes), 0)
+    tiles = [jnp.concatenate([a[8 * t:8 * t + 8], jnp.where(c_io == r_io + 8 * t, 1.0, 0.0).astype(F32)], axis=1)
+             for t in range(count)]
+    def wide(v):
+        return v if lanes == 128 else jnp.concatenate([v] * (lanes // 128), axis=1)
+    for g in range(count):
+        cols = {t: [jnp.broadcast_to(tiles[t][:, 8 * g + k:8 * g + k + 1], (8, 128)) for k in range(8)]
+                for t in range(g, count)}
+        piv = [[jnp.broadcast_to(cols[g][b][i:i + 1, :], (8, 128)) for b in range(i + 1)] for i in range(8)]
+        rows = [jnp.broadcast_to(tiles[g][k:k + 1, :], (8, lanes)) for k in range(8)]
+        for k in range(8):
+            d = lax.rsqrt(piv[k][k])
+            low = {i: piv[i][k] * d for i in range(k + 1, 8)}
+            for i in range(k + 1, 8):
+                for b in range(k + 1, i + 1):
+                    piv[i][b] = piv[i][b] - low[i] * low[b]
+            rows[k] = rows[k] * wide(d)
+            for i in range(k + 1, 8):
+                rows[i] = rows[i] - wide(low[i]) * rows[k]
+            for t in range(g + 1, count):
+                cols[t][k] = cols[t][k] * d
+                for i in range(k + 1, 8):
+                    cols[t][i] = cols[t][i] - low[i] * cols[t][k]
+                tiles[t] = tiles[t] - wide(cols[t][k]) * rows[k]
+        new = rows[0]
+        for k in range(1, 8):
+            new = jnp.where(sub == k, rows[k], new)
+        tiles[g] = new
+    w = jnp.concatenate(tiles, axis=0)
+    return w[:, :n], w[:, n:]
+
+
+def split(v):
+    hi = v.astype(BF16)
+    return hi, (v - hi.astype(F32)).astype(BF16)
+
+
+def mm(a, b, dims):
+    ah, al = split(a); bh, bl = split(b)
+    dot = lambda p, q: lax.dot_general(p, q, (dims, ((), ())), preferred_element_type=F32)
+    return dot(ah, bh) + (dot(ah, bl) + dot(al, bh))
+
+
+def hi(a, b, dims):
+    return lax.dot_general(a, b, (dims, ((), ())), precision=lax.Precision.HIGHEST, preferred_element_type=F32)
+
+
+def factor_kernel(n, g_ref, r_ref, l_ref, d_ref, w):
+    m = g_ref.shape[0]
+    nb = m // n
+    w[...] = g_ref[...]
+    r_io = lax.broadcasted_iota(jnp.int32, (n, n), 0)
+    c_io = lax.broadcasted_iota(jnp.int32, (n, n), 1)
+    xs = []; ups = {}
+    for k in range(nb):
+        s = slice(k * n, (k + 1) * n)
+        u, v = eliminate(w[s, s], n)
+        l_ref[s, s] = jnp.where(r_io >= c_io, u.T, 0.0)
+        if k + 1 < nb:
+            rest = slice((k + 1) * n, m)
+            up = hi(v, w[s, rest], ((1,), (0,)))
+            w[rest, rest] = w[rest, rest] - hi(up, up, ((0,), (0,)))
+            l_ref[rest, s] = up.T
+            l_ref[s, rest] = jnp.zeros((n, m - (k + 1) * n), F32)
+            ups[k] = up
+        acc = r_ref[s, :]
+        for j in range(k):
+            acc = acc - mm(ups[j][:, (k - j - 1) * n:(k - j) * n], xs[j], ((0,), (0,)))
+        x = mm(v, acc, ((1,), (0,)))
+        xs.append(x)
+        d_ref[s, :] = x.astype(BF16)
+
+
 def shards(sides, basis_cols, snapshots):
     ny, nz, nx, points = sides
     own_points = basis_cols.shape[0] // nx
@@ -224,7 +302,7 @@
             jax.ShapeDtypeStruct((snaps, snaps), F32),
             jax.ShapeDtypeStruct((snaps, own_points), F32),
         ),
-        in_specs=[pl.BlockSpec(memory_space=pl.ANY)] * 2,
+        in_specs=[pl.BlockSpec(memory_space=pltpu.HBM)] * 2,
         out_specs=(pl.BlockSpec(memory_space=pltpu.VMEM),) * 3,
         scratch_shapes=[
             pltpu.VMEM(basis_cols.shape, BF16),
@@ -253,12 +331,20 @@
             dma(()), dma(()),
         ],
         compiler_params=pltpu.CompilerParams(
-            collective_id=0, has_side_effects=True, vmem_limit_bytes=48 << 20
+            collective_id=0, has_side_effects=True, vmem_limit_bytes=60 << 20
         ),
         name="exchange",
     )(basis_cols, snapshots)
-    factor = jnp.linalg.cholesky(gram)
-    directions = lax.linalg.triangular_solve(factor, residual, left_side=True, lower=True).astype(BF16)
+    factor, directions = pl.pallas_call(
+        functools.partial(factor_kernel, 64),
+        out_shape=(
+            jax.ShapeDtypeStruct((snaps, snaps), F32),
+            jax.ShapeDtypeStruct((snaps, own_points), BF16),
+        ),
+        scratch_shapes=[pltpu.VMEM((snaps, snaps), F32)],
+        compiler_params=pltpu.CompilerParams(vmem_limit_bytes=32 << 20),
+        name="factor",
+    )(gram, residual)
     return (coefficients, factor, directions)
 
 

time: 138 us -> 86.7 us (0.63)
  other arithmetic: 55.4 us -> 0 us
  Pallas kernels: 70.3 us -> 82 us
  local copies, waits for them, and re-layouts: 8.17 us -> 3.84 us
  matrix products: 2.32 us -> 0 us
    another operation x10 -> x0, other arithmetic: 55.3 us -> none  [the longest x6 34.1 us: shards(): factor = jnp.linalg.cholesky(gram)]
    pallas_call x0 -> x1, Pallas kernels: none -> 10.6 us  [shards(): pl.pallas_call(functools.partial(factor_kernel, 64), out_shape=(jax.Shape...]
    another operation x9 -> x0, local copies, waits for them, and re-layouts: 4.15 us -> none
    another operation x5 -> x0, matrix products: 2.32 us -> none  [the longest x3 1.85 us: shards(): lax.linalg.triangular_solve(factor, residual, left_side=True, lower=True)]
where the time goes in v2:
time: 86.7 us; the launch traced here: 86.4 us
  Pallas kernels  82 us (95%)
  local copies, waits for them, and re-layouts  3.84 us (4%)
    pallas_call x1, Pallas kernels, shards(): pl.pallas_call(functools.partial(exchange, sides), out_shape=(jax.ShapeDt...  71.3 us
    pallas_call x1, Pallas kernels, shards(): pl.pallas_call(functools.partial(factor_kernel, 64), out_shape=(jax.Shape...  10.6 us
    unnamed x5, local copies, waits for them, and re-layouts  3.84 us

profile of v2, /device:TPU:1, one launch (start us, length us, event | category | flops | bytes accessed | tf_op | source)
XLA Modules:
  0.0 86.4 jit_solution(4425031863422588909)
XLA Ops:
  0.6 71.3 %exchange.1 = (f32[256,256]{1,0:T(8,128)}, f32[256,256]{1,0:T(8,128)}, f32[256,1024]{1,0:T(8,128)}) custom-call(bf16[4096,256]{1,0:T(8,128)(2,1)} %b_hbm.1, bf16[256,4096]{1,0:T(8,128)(2,1)} %s_hbm.1), custom_call_target="tpu_custom_call" | custom-call | tf_op jit(solution)/shard_map/exchange/pallas_call | solution.py:298
  72.0 0.0 copy-start
  72.0 1.2 %copy-done = f32[256,1024]{1,0:T(8,128)S(1)} copy-done((f32[256,1024]{1,0:T(8,128)S(1)}, f32[256,1024]{1,0:T(8,128)}, u32[]{:S(2)}) %copy-start) | copy-done | bytes 1048600
  73.2 0.0 copy-start.1
  73.2 0.9 %copy-done.1 = f32[256,256]{1,0:T(8,128)S(1)} copy-done((f32[256,256]{1,0:T(8,128)S(1)}, f32[256,256]{1,0:T(8,128)}, u32[]{:S(2)}) %copy-start.1) | copy-done | bytes 262168
  74.2 10.6 %factor.1 = (f32[256,256]{1,0:T(8,128)}, bf16[256,1024]{1,0:T(8,128)(2,1)}) custom-call(f32[256,256]{1,0:T(8,128)S(1)} %copy-done.1, f32[256,1024]{1,0:T(8,128)S(1)} %copy-done), custom_call_target="tpu_custom_call" | custom-call | tf_op jit(solution)/shard_map/factor/pallas_call | solution.py:338
  84.8 1.7 %copy.6 = f32[256,256]{1,0:T(8,128)} copy(f32[256,256]{1,0:T(8,128)} %get-tuple-element.16) | data formatting | bytes 524288
Async XLA Ops:
  72.0 1.2 %copy-start = (f32[256,1024]{1,0:T(8,128)S(1)}, f32[256,1024]{1,0:T(8,128)}, u32[]{:S(2)}) copy-start(f32[256,1024]{1,0:T(8,128)} %get-tuple-element.10.r_ref) | copy-start | bytes 3145732
  73.2 0.9 %copy-start.1 = (f32[256,256]{1,0:T(8,128)S(1)}, f32[256,256]{1,0:T(8,128)}, u32[]{:S(2)}) copy-start(f32[256,256]{1,0:T(8,128)} %get-tuple-element.9.g_ref) | copy-start | bytes 786436

commit v3 on v2

v3 whole, which is shorter than its diff:
```python
import functools
import math

import jax
import jax.numpy as jnp
from jax import lax
from jax.experimental import pallas as pl
from jax.experimental.pallas import tpu as pltpu
from jax.sharding import PartitionSpec as P

RANK = 1024
SIDE_Y = 8
MESH = pl.DeviceIdType.MESH
F32 = jnp.float32
BF16 = jnp.bfloat16
HALF = 128


def exchange(sides, b_hbm, s_hbm, coef_o, gram_o, res_o, bv, sv, bfull, qfull, cbuf, pbuf, pbuf2, gbuf,
             core_in, part, rs_in, ar_in, x_in, load_sem, bx_s, bx_r, core_s, core_r, rs_s, rs_r, ar_s, ar_r, x_s, x_r,
             ag_s, ag_r, out_s, out_r, cag_s, cag_r, cout_s, cout_r):
    ny, nz, nx, points = sides
    row, x = lax.axis_index("rows"), lax.axis_index("cols")
    z, y, c = row // (2 * ny), (row // 2) % ny, row % 2
    own_points = b_hbm.shape[0] // nx
    ring = ny
    rows = HALF // ring

    def device(z, y, c, x):
        return ((z * ny + y) * 2 + c, x)

    mate = device(z, y, 1 - c, x)
    far = sorted(range(1, ring), key=lambda k: -min(k, ring - k))
    one, two = jnp.where(c == 0, y, z), jnp.where(c == 0, z, y)
    one_peers = [lax.rem(one + k, ring) for k in far]
    two_peers = [lax.rem(two + k, ring) for k in far]
    x_peers = [lax.rem(x + k, nx) for k in sorted(range(1, nx), key=lambda k: -min(k, nx - k))]

    def along_one(t):
        return device(jnp.where(c == 0, z, t), jnp.where(c == 0, t, y), c, x)

    def along_two(t):
        return device(jnp.where(c == 0, t, z), jnp.where(c == 0, y, t), c, x)

    def along_x(t):
        return device(z, y, c, t)

    def remote(src, dst, send, recv, dev):
        return pltpu.make_async_remote_copy(
            src_ref=src, dst_ref=dst, send_sem=send, recv_sem=recv, device_id=dev, device_id_type=MESH
        )

    pending = []

    def send(*args):
        copy = remote(*args)
        copy.start()
        pending.append(copy)

    def arrived(ref, sem):
        remote(ref, ref, load_sem.at[3], sem, mate).wait_recv()

    load_b = pltpu.make_async_copy(b_hbm, bv, load_sem.at[0])
    load_s = pltpu.make_async_copy(s_hbm, sv, load_sem.at[1])
    load_b.start()
    load_s.start()

    barrier = pltpu.get_barrier_semaphore()
    peers = [mate] + [along_one(t) for t in one_peers] + [along_two(t) for t in two_peers]
    peers += [along_x(t) for t in x_peers]
    for peer in peers:
        pl.semaphore_signal(barrier, inc=1, device_id=peer, device_id_type=MESH)
    pl.semaphore_wait(barrier, len(peers))

    for t in x_peers:
        send(b_hbm.at[pl.ds(t * own_points, own_points)], bfull.at[x], bx_s.at[t], bx_r.at[x], along_x(t))
    load_own = pltpu.make_async_copy(b_hbm.at[pl.ds(x * own_points, own_points)], bfull.at[x], load_sem.at[2])
    load_own.start()

    load_b.wait()
    load_s.wait()
    steps = 4
    depth = b_hbm.shape[0] // steps
    total = None
    for k in range(steps):
        piece = jnp.dot(sv[:, k * depth:(k + 1) * depth], bv[k * depth:(k + 1) * depth, :],
                        preferred_element_type=F32)
        total = piece if total is None else total + piece

    chunk = pl.ds(pl.multiple_of(one * rows, rows), rows)
    half = pl.ds(pl.multiple_of(c * HALF, HALF), HALF)
    other = pl.ds(pl.multiple_of((1 - c) * HALF, HALF), HALF)

    def half_chunk(t):
        return pl.ds(pl.multiple_of(c * HALF + t * rows, rows), rows)

    def row_sum(phase, buf, value):
        buf[...] = value
        send(buf.at[other], core_in.at[phase], core_s.at[phase], core_r.at[phase], mate)
        arrived(core_in.at[phase], core_r.at[phase])
        part[phase] = buf[half, :] + core_in[phase]
        for t in one_peers:
            send(part.at[phase, pl.ds(pl.multiple_of(t * rows, rows), rows)], rs_in.at[phase, one],
                 rs_s.at[phase, t], rs_r.at[phase, one], along_one(t))
        rs_in[phase, one] = part[phase, chunk, :]
        for t in one_peers:
            arrived(rs_in.at[phase, t], rs_r.at[phase, t])
        got = rs_in[phase, 0]
        for i in range(1, ring):
            got = got + rs_in[phase, i]
        ar_in[phase, two] = got
        for t in two_peers:
            send(ar_in.at[phase, two], ar_in.at[phase, two], ar_s.at[phase, t], ar_r.at[phase, two], along_two(t))
        for t in two_peers:
            arrived(ar_in.at[phase, t], ar_r.at[phase, t])
        got = ar_in[phase, 0]
        for i in range(1, ring):
            got = got + ar_in[phase, i]
        return got

    own = row_sum(0, pbuf, total) * (math.sqrt(RANK) / points)
    mine = half_chunk(one)
    qfull[x, mine, :] = own.astype(BF16)
    for t in x_peers:
        send(qfull.at[x, mine], qfull.at[x, mine], x_s.at[0, t], x_r.at[0, x], along_x(t))
    cbuf[mine, :] = own
    for t in x_peers:
        arrived(qfull.at[t, mine], x_r.at[0, t])
    for t in one_peers:
        send(qfull.at[:, mine], qfull.at[:, mine], ag_s.at[0, t], ag_r.at[0, one], along_one(t))
    for t in one_peers:
        send(cbuf.at[mine], cbuf.at[mine], cag_s.at[t], cag_r.at[one], along_one(t))
    for t in one_peers:
        arrived(qfull.at[:, half_chunk(t)], ag_r.at[0, t])
    send(qfull.at[:, half], qfull.at[:, half], out_s.at[0], out_r.at[0], mate)
    for t in one_peers:
        arrived(cbuf.at[half_chunk(t)], cag_r.at[t])
    send(cbuf.at[half], cbuf.at[half], cout_s, cout_r, mate)
    arrived(qfull.at[:, other], out_r.at[0])

    def from_modes(t):
        return lax.dot_general(qfull[t], bfull[t], (((1,), (1,)), ((), ())), preferred_element_type=F32)

    load_own.wait()
    recon = from_modes(x)
    for t in reversed(x_peers):
        arrived(bfull.at[t], bx_r.at[t])
        recon = recon + from_modes(t)
    own_snaps = sv[:, pl.ds(pl.multiple_of(x * own_points, own_points), own_points)].astype(F32)
    residual = own_snaps - recon * (1.0 / math.sqrt(RANK))
    gram = lax.dot_general(residual, residual, (((1,), (1,)), ((), ())), precision=lax.Precision.HIGHEST,
                           preferred_element_type=F32) * (1.0 / points)
    res_o[...] = residual
    got = row_sum(1, pbuf2, gram)
    x_in[x] = got
    for t in x_peers:
        send(x_in.at[x], x_in.at[x], x_s.at[1, t], x_r.at[1, x], along_x(t))
    arrived(cbuf.at[other], cout_r)
    coef_o[...] = cbuf[...].T
    for t in x_peers:
        arrived(x_in.at[t], x_r.at[1, t])
    got = x_in[0]
    for i in range(1, nx):
        got = got + x_in[i]
    gbuf[mine, :] = got
    for t in one_peers:
        send(gbuf.at[mine], gbuf.at[mine], ag_s.at[1, t], ag_r.at[1, one], along_one(t))
    for t in one_peers:
        arrived(gbuf.at[half_chunk(t)], ag_r.at[1, t])
    send(gbuf.at[half], gbuf.at[half], out_s.at[1], out_r.at[1], mate)
    gram_o[half, :] = gbuf[half, :]
    arrived(gbuf.at[other], out_r.at[1])
    gram_o[other, :] = gbuf[other, :]
    for copy in pending:
        copy.wait_send()


def eliminate(a, n):
    lanes = 2 * n
    count = n // 8
    r_io = lax.broadcasted_iota(jnp.int32, (8, n), 0)
    c_io = lax.broadcasted_iota(jnp.int32, (8, n), 1)
    sub = lax.broadcasted_iota(jnp.int32, (8, lanes), 0)
    tiles = [jnp.concatenate([a[8 * t:8 * t + 8], jnp.where(c_io == r_io + 8 * t, 1.0, 0.0).astype(F32)], axis=1)
             for t in range(count)]
    def wide(v):
        return v if lanes == 128 else jnp.concatenate([v] * (lanes // 128), axis=1)
    for g in range(count):
        cols = {t: [jnp.broadcast_to(tiles[t][:, 8 * g + k:8 * g + k + 1], (8, 128)) for k in range(8)]
                for t in range(g, count)}
        piv = [[jnp.broadcast_to(cols[g][b][i:i + 1, :], (8, 128)) for b in range(i + 1)] for i in range(8)]
        rows = [jnp.broadcast_to(tiles[g][k:k + 1, :], (8, lanes)) for k in range(8)]
        for k in range(8):
            d = lax.rsqrt(piv[k][k])
            low = {i: piv[i][k] * d for i in range(k + 1, 8)}
            for i in range(k + 1, 8):
                for b in range(k + 1, i + 1):
                    piv[i][b] = piv[i][b] - low[i] * low[b]
            rows[k] = rows[k] * wide(d)
            for i in range(k + 1, 8):
                rows[i] = rows[i] - wide(low[i]) * rows[k]
            for t in range(g + 1, count):
                cols[t][k] = cols[t][k] * d
                for i in range(k + 1, 8):
                    cols[t][i] = cols[t][i] - low[i] * cols[t][k]
                tiles[t] = tiles[t] - wide(cols[t][k]) * rows[k]
        new = rows[0]
        for k in range(1, 8):
            new = jnp.where(sub == k, rows[k], new)
        tiles[g] = new
    w = jnp.concatenate(tiles, axis=0)
    return w[:, :n], w[:, n:]


def split(v):
    hi = v.astype(BF16)
    return hi, (v - hi.astype(F32)).astype(BF16)


def mm(a, b, dims):
    ah, al = split(a); bh, bl = split(b)
    dot = lambda p, q: lax.dot_general(p, q, (dims, ((), ())), preferred_element_type=F32)
    return dot(ah, bh) + (dot(ah, bl) + dot(al, bh))


def hi(a, b, dims):
    return lax.dot_general(a, b, (dims, ((), ())), precision=lax.Precision.HIGHEST, preferred_element_type=F32)


def factor_kernel(n, g_ref, r_ref, c_ref, c_out, l_out, d_out, w, low, dirs, sems):
    m = g_ref.shape[0]
    count = m // n
    pending = []

    def put(src, dst, k):
        copy = pltpu.make_async_copy(src, dst, sems.at[k])
        copy.start()
        pending.append(copy)

    put(c_ref, c_out, 0)
    w[...] = g_ref[...]
    r_io = lax.broadcasted_iota(jnp.int32, (n, n), 0)
    c_io = lax.broadcasted_iota(jnp.int32, (n, n), 1)
    xs, ups = [], []
    for k in range(count):
        s = slice(k * n, (k + 1) * n)
        u, v = eliminate(w[s, s], n)
        low[s, s] = jnp.where(r_io >= c_io, u.T, 0.0)
        if k + 1 < count:
            rest = slice((k + 1) * n, m)
            up = hi(v, w[s, rest], ((1,), (0,)))
            w[rest, rest] = w[rest, rest] - hi(up, up, ((0,), (0,)))
            low[rest, s] = up.T
            low[s, rest] = jnp.zeros((n, m - (k + 1) * n), F32)
            ups.append(up)
        put(low.at[s], l_out.at[s], 1 + k)
        acc = r_ref[s, :]
        for j in range(k):
            acc = acc - mm(ups[j][:, (k - j - 1) * n:(k - j) * n], xs[j], ((0,), (0,)))
        x = mm(v, acc, ((1,), (0,)))
        xs.append(x)
        dirs[s, :] = x.astype(BF16)
        put(dirs.at[s], d_out.at[s], 1 + count + k)
    for copy in pending:
        copy.wait()


def shards(sides, basis_cols, snapshots):
    ny, nz, nx, points = sides
    own_points = basis_cols.shape[0] // nx
    modes = basis_cols.shape[1]
    snaps = snapshots.shape[0]
    n = max(ny, nz)
    dma = pltpu.SemaphoreType.DMA
    chunk = HALF // n
    coefficients, gram, residual = pl.pallas_call(
        functools.partial(exchange, sides),
        out_shape=(
            jax.ShapeDtypeStruct((modes, snaps), F32),
            jax.ShapeDtypeStruct((snaps, snaps), F32),
            jax.ShapeDtypeStruct((snaps, own_points), F32),
        ),
        in_specs=[pl.BlockSpec(memory_space=pltpu.HBM)] * 2,
        out_specs=(pl.BlockSpec(memory_space=pltpu.VMEM),) * 3,
        scratch_shapes=[
            pltpu.VMEM(basis_cols.shape, BF16),
            pltpu.VMEM(snapshots.shape, BF16),
            pltpu.VMEM((nx, own_points, modes), BF16),
            pltpu.VMEM((nx, snaps, modes), BF16),
            pltpu.VMEM((snaps, modes), F32),
            pltpu.VMEM((snaps, modes), F32),
            pltpu.VMEM((snaps, snaps), F32),
            pltpu.VMEM((snaps, snaps), F32),
            pltpu.VMEM((2, HALF, snaps), F32),
            pltpu.VMEM((2, HALF, snaps), F32),
            pltpu.VMEM((2, n, chunk, snaps), F32),
            pltpu.VMEM((2, n, chunk, snaps), F32),
            pltpu.VMEM((nx, chunk, snaps), F32),
            dma((4,)),
            dma((nx,)), dma((nx,)),
            dma((2,)), dma((2,)),
            dma((2, n)), dma((2, n)),
            dma((2, n)), dma((2, n)),
            dma((2, nx)), dma((2, nx)),
            dma((2, n)), dma((2, n)),
            dma((2,)), dma((2,)),
            dma((n,)), dma((n,)),
            dma(()), dma(()),
        ],
        compiler_params=pltpu.CompilerParams(
            collective_id=0, has_side_effects=True, vmem_limit_bytes=52 << 20
        ),
        name="exchange",
    )(basis_cols, snapshots)
    block = 64
    coefficients, factor, directions = pl.pallas_call(
        functools.partial(factor_kernel, block),
        out_shape=(
            jax.ShapeDtypeStruct((modes, snaps), F32),
            jax.ShapeDtypeStruct((snaps, snaps), F32),
            jax.ShapeDtypeStruct((snaps, own_points), BF16),
        ),
        in_specs=[pl.BlockSpec(memory_space=pltpu.VMEM)] * 3,
        out_specs=(pl.BlockSpec(memory_space=pl.ANY),) * 3,
        scratch_shapes=[
            pltpu.VMEM((snaps, snaps), F32),
            pltpu.VMEM((snaps, snaps), F32),
            pltpu.VMEM((snaps, own_points), BF16),
            dma((1 + 2 * (snaps // block),)),
        ],
        compiler_params=pltpu.CompilerParams(vmem_limit_bytes=32 << 20),
        name="factor",
    )(gram, residual, coefficients)
    return (coefficients, factor, directions)


def solution(mesh):
    rows, cols = mesh.shape["rows"], mesh.shape["cols"]
    placed = (P("rows", "cols"), P(None, "rows"))

    def whole(basis_cols, snapshots):
        sides = (SIDE_Y, rows // (2 * SIDE_Y), cols, basis_cols.shape[0])
        return jax.shard_map(
            functools.partial(shards, sides),
            mesh=mesh,
            in_specs=placed,
            out_specs=(P("cols", None), P(), P(None, ("rows", "cols"))),
            check_vma=False,
        )(basis_cols, snapshots)

    return whole
```

time: 86.7 us -> 84.1 us (0.970)
  local copies, waits for them, and re-layouts: 3.84 us -> 0 us
  Pallas kernels: 82 us -> 83.4 us
    unnamed x5 -> x0, local copies, waits for them, and re-layouts: 3.84 us -> none
    pallas_call x1, Pallas kernels: 71.3 us -> 72.8 us  [shards(): pl.pallas_call(functools.partial(exchange, sides), out_shape=(jax.ShapeDt...]
where the time goes in v3:
time: 84.1 us; the launch traced here: 84 us
  Pallas kernels  83.4 us (99%)
    pallas_call x1, Pallas kernels, shards(): pl.pallas_call(functools.partial(exchange, sides), out_shape=(jax.ShapeDt...  72.8 us
    pallas_call x1, Pallas kernels, shards(): pl.pallas_call(functools.partial(factor_kernel, block), out_shape=(jax.Sh...  10.6 us

profile of v3, /device:TPU:1, one launch (start us, length us, event | category | flops | bytes accessed | tf_op | source)
XLA Modules:
  0.0 84.0 jit_solution(6077918461160990742)
XLA Ops:
  0.6 72.8 %exchange.1 = (f32[256,256]{1,0:T(8,128)S(1)}, f32[256,256]{1,0:T(8,128)S(1)}, f32[256,1024]{1,0:T(8,128)S(1)}) custom-call(bf16[4096,256]{1,0:T(8,128)(2,1)} %b_hbm.1, bf16[256,4096]{1,0:T(8,128)(2,1)} %s_hbm.1), custom_call_target="tpu_custom_call" | custom-call | tf_op jit(solution)/shard_map/exchange/pallas_call | solution.py:276
  73.4 10.6 %factor.1 = (f32[256,256]{1,0:T(8,128)}, f32[256,256]{1,0:T(8,128)}, bf16[256,1024]{1,0:T(8,128)(2,1)}) custom-call(f32[256,256]{1,0:T(8,128)S(1)} %get-tuple-element.6.g_ref, f32[256,1024]{1,0:T(8,128)S(1)} %get-tuple-element.7.r_ref, f32[256,256]{1,0:T(8,128)S(1)} %get-tuple-element.8.c_ref), custom_call_target="tpu_custom_call" | custom-call | tf_op jit(solution)/shard_map/factor/pallas_call | solution.py:316

commit v4 on v3

--- a/solution.py
+++ b/solution.py
@@ -14,6 +14,7 @@
 F32 = jnp.float32
 BF16 = jnp.bfloat16
 HALF = 128
+SHARES = (7, 2, 4, 3)
 
 
 def exchange(sides, b_hbm, s_hbm, coef_o, gram_o, res_o, bv, sv, bfull, qfull, cbuf, pbuf, pbuf2, gbuf,
@@ -72,8 +73,15 @@
         pl.semaphore_signal(barrier, inc=1, device_id=peer, device_id_type=MESH)
     pl.semaphore_wait(barrier, len(peers))
 
-    for t in x_peers:
-        send(b_hbm.at[pl.ds(t * own_points, own_points)], bfull.at[x], bx_s.at[t], bx_r.at[x], along_x(t))
+    spans = [(sum(SHARES[:k]) * own_points // 16, SHARES[k] * own_points // 16) for k in range(len(SHARES))]
+
+    def send_basis(k):
+        start, size = spans[k]
+        for t in x_peers:
+            send(b_hbm.at[pl.ds(t * own_points + start, size)], bfull.at[x, pl.ds(start, size)], bx_s.at[k, t],
+                 bx_r.at[k, x], along_x(t))
+
+    send_basis(0)
     load_own = pltpu.make_async_copy(b_hbm.at[pl.ds(x * own_points, own_points)], bfull.at[x], load_sem.at[2])
     load_own.start()
 
@@ -123,6 +131,7 @@
     qfull[x, mine, :] = own.astype(BF16)
     for t in x_peers:
         send(qfull.at[x, mine], qfull.at[x, mine], x_s.at[0, t], x_r.at[0, x], along_x(t))
+    send_basis(1)
     cbuf[mine, :] = own
     for t in x_peers:
         arrived(qfull.at[t, mine], x_r.at[0, t])
@@ -130,12 +139,11 @@
         send(qfull.at[:, mine], qfull.at[:, mine], ag_s.at[0, t], ag_r.at[0, one], along_one(t))
     for t in one_peers:
         send(cbuf.at[mine], cbuf.at[mine], cag_s.at[t], cag_r.at[one], along_one(t))
+    send_basis(2)
     for t in one_peers:
         arrived(qfull.at[:, half_chunk(t)], ag_r.at[0, t])
     send(qfull.at[:, half], qfull.at[:, half], out_s.at[0], out_r.at[0], mate)
-    for t in one_peers:
-        arrived(cbuf.at[half_chunk(t)], cag_r.at[t])
-    send(cbuf.at[half], cbuf.at[half], cout_s, cout_r, mate)
+    send_basis(3)
     arrived(qfull.at[:, other], out_r.at[0])
 
     def from_modes(t):
@@ -144,13 +152,17 @@
     load_own.wait()
     recon = from_modes(x)
     for t in reversed(x_peers):
-        arrived(bfull.at[t], bx_r.at[t])
+        for k, (start, size) in enumerate(spans):
+            arrived(bfull.at[t, pl.ds(start, size)], bx_r.at[k, t])
         recon = recon + from_modes(t)
     own_snaps = sv[:, pl.ds(pl.multiple_of(x * own_points, own_points), own_points)].astype(F32)
     residual = own_snaps - recon * (1.0 / math.sqrt(RANK))
     gram = lax.dot_general(residual, residual, (((1,), (1,)), ((), ())), precision=lax.Precision.HIGHEST,
                            preferred_element_type=F32) * (1.0 / points)
     res_o[...] = residual
+    for t in one_peers:
+        arrived(cbuf.at[half_chunk(t)], cag_r.at[t])
+    send(cbuf.at[half], cbuf.at[half], cout_s, cout_r, mate)
     got = row_sum(1, pbuf2, gram)
     x_in[x] = got
     for t in x_peers:
@@ -297,7 +309,7 @@
             pltpu.VMEM((2, n, chunk, snaps), F32),
             pltpu.VMEM((nx, chunk, snaps), F32),
             dma((4,)),
-            dma((nx,)), dma((nx,)),
+            dma((len(SHARES), nx)), dma((len(SHARES), nx)),
             dma((2,)), dma((2,)),
             dma((2, n)), dma((2, n)),
             dma((2, n)), dma((2, n)),

time: 84.1 us -> 77.2 us (0.918)
  Pallas kernels: 83.4 us -> 76.5 us
    pallas_call x1, Pallas kernels: 72.8 us -> 65.9 us  [shards(): pl.pallas_call(functools.partial(exchange, sides), out_shape=(jax.ShapeDt...]
where the time goes in v4:
time: 77.2 us; the launch traced here: 77.1 us
  Pallas kernels  76.5 us (99%)
    pallas_call x1, Pallas kernels, shards(): pl.pallas_call(functools.partial(exchange, sides), out_shape=(jax.ShapeDt...  65.9 us
    pallas_call x1, Pallas kernels, shards(): pl.pallas_call(functools.partial(factor_kernel, block), out_shape=(jax.Sh...  10.6 us

profile of v4, /device:TPU:1, one launch (start us, length us, event | category | flops | bytes accessed | tf_op | source)
XLA Modules:
  0.0 77.1 jit_solution(9047648708099334409)
XLA Ops:
  0.6 65.9 %exchange.1 = (f32[256,256]{1,0:T(8,128)S(1)}, f32[256,256]{1,0:T(8,128)S(1)}, f32[256,1024]{1,0:T(8,128)S(1)}) custom-call(bf16[4096,256]{1,0:T(8,128)(2,1)} %b_hbm.1, bf16[256,4096]{1,0:T(8,128)(2,1)} %s_hbm.1), custom_call_target="tpu_custom_call" | custom-call | tf_op jit(solution)/shard_map/exchange/pallas_call | solution.py:288
  66.5 10.6 %factor.1 = (f32[256,256]{1,0:T(8,128)}, f32[256,256]{1,0:T(8,128)}, bf16[256,1024]{1,0:T(8,128)(2,1)}) custom-call(f32[256,256]{1,0:T(8,128)S(1)} %get-tuple-element.6.g_ref, f32[256,1024]{1,0:T(8,128)S(1)} %get-tuple-element.7.r_ref, f32[256,256]{1,0:T(8,128)S(1)} %get-tuple-element.8.c_ref), custom_call_target="tpu_custom_call" | custom-call | tf_op jit(solution)/shard_map/factor/pallas_call | solution.py:328

commit v5 on v4

--- a/solution.py
+++ b/solution.py
@@ -187,35 +187,41 @@
         copy.wait_send()
 
 
-def eliminate(a, n):
+def eliminate(a, n, buf):
     lanes = 2 * n
     count = n // 8
     r_io = lax.broadcasted_iota(jnp.int32, (8, n), 0)
     c_io = lax.broadcasted_iota(jnp.int32, (8, n), 1)
     sub = lax.broadcasted_iota(jnp.int32, (8, lanes), 0)
-    tiles = [jnp.concatenate([a[8 * t:8 * t + 8], jnp.where(c_io == r_io + 8 * t, 1.0, 0.0).astype(F32)], axis=1)
+    tiles = [jnp.concatenate([jnp.where(c_io == r_io + 8 * t, 1.0, 0.0).astype(F32), a[8 * t:8 * t + 8]], axis=1)
              for t in range(count)]
-    def wide(v):
-        return v if lanes == 128 else jnp.concatenate([v] * (lanes // 128), axis=1)
+
+    def spread(v):
+        return jnp.broadcast_to(v, (8, lanes))
+
     for g in range(count):
-        cols = {t: [jnp.broadcast_to(tiles[t][:, 8 * g + k:8 * g + k + 1], (8, 128)) for k in range(8)]
-                for t in range(g, count)}
-        piv = [[jnp.broadcast_to(cols[g][b][i:i + 1, :], (8, 128)) for b in range(i + 1)] for i in range(8)]
-        rows = [jnp.broadcast_to(tiles[g][k:k + 1, :], (8, lanes)) for k in range(8)]
+        base, slot = n + 8 * g, g % 2
+        cols = {t: [spread(tiles[t][:, base + k:base + k + 1]) for k in range(8)] for t in range(g, count)}
+        for k in range(8):
+            buf[slot, k] = cols[g][k]
+        buf[slot, 8] = tiles[g]
+        piv = [[spread(buf[slot, b, i:i + 1, :]) for b in range(i + 1)] for i in range(8)]
+        rows = [spread(buf[slot, 8, k:k + 1, :]) for k in range(8)]
         for k in range(8):
             d = lax.rsqrt(piv[k][k])
-            low = {i: piv[i][k] * d for i in range(k + 1, 8)}
+            inv = pl.reciprocal(piv[k][k], approx=True)
             for i in range(k + 1, 8):
                 for b in range(k + 1, i + 1):
-                    piv[i][b] = piv[i][b] - low[i] * low[b]
-            rows[k] = rows[k] * wide(d)
+                    piv[i][b] = piv[i][b] - (piv[i][k] * piv[b][k]) * inv
+            low = {i: piv[i][k] * d for i in range(k + 1, 8)}
+            rows[k] = rows[k] * d
             for i in range(k + 1, 8):
-                rows[i] = rows[i] - wide(low[i]) * rows[k]
+                rows[i] = rows[i] - low[i] * rows[k]
             for t in range(g + 1, count):
                 cols[t][k] = cols[t][k] * d
                 for i in range(k + 1, 8):
                     cols[t][i] = cols[t][i] - low[i] * cols[t][k]
-                tiles[t] = tiles[t] - wide(cols[t][k]) * rows[k]
+                tiles[t] = tiles[t] - cols[t][k] * rows[k]
         new = rows[0]
         for k in range(1, 8):
             new = jnp.where(sub == k, rows[k], new)
@@ -224,24 +230,29 @@
     return w[:, :n], w[:, n:]
 
 
+NN, NT = ((1,), (0,)), ((1,), (1,))
+
+
 def split(v):
-    hi = v.astype(BF16)
-    return hi, (v - hi.astype(F32)).astype(BF16)
-
-
-def mm(a, b, dims):
-    ah, al = split(a); bh, bl = split(b)
-    dot = lambda p, q: lax.dot_general(p, q, (dims, ((), ())), preferred_element_type=F32)
+    high = v.astype(BF16)
+    return high, (v - high.astype(F32)).astype(BF16)
+
+
+def three(a, b, dims):
+    (ah, al), (bh, bl) = split(a), split(b)
+
+    def dot(p, q):
+        return lax.dot_general(p, q, (dims, ((), ())), preferred_element_type=F32)
+
     return dot(ah, bh) + (dot(ah, bl) + dot(al, bh))
 
 
-def hi(a, b, dims):
+def full(a, b, dims):
     return lax.dot_general(a, b, (dims, ((), ())), precision=lax.Precision.HIGHEST, preferred_element_type=F32)
 
 
-def factor_kernel(n, g_ref, r_ref, c_ref, c_out, l_out, d_out, w, low, dirs, sems):
-    m = g_ref.shape[0]
-    count = m // n
+def factor_kernel(n, g_ref, r_ref, c_ref, c_out, l_out, d_out, factor, dirs, buf, sems):
+    count = g_ref.shape[0] // n
     pending = []
 
     def put(src, dst, k):
@@ -249,30 +260,33 @@
         copy.start()
         pending.append(copy)
 
+    def span(k):
+        return slice(k * n, (k + 1) * n)
+
     put(c_ref, c_out, 0)
-    w[...] = g_ref[...]
     r_io = lax.broadcasted_iota(jnp.int32, (n, n), 0)
     c_io = lax.broadcasted_iota(jnp.int32, (n, n), 1)
-    xs, ups = [], []
+    block = {(i, k): g_ref[span(i), span(k)] for k in range(count) for i in range(k, count)}
+    low, xs = {}, []
     for k in range(count):
-        s = slice(k * n, (k + 1) * n)
-        u, v = eliminate(w[s, s], n)
-        low[s, s] = jnp.where(r_io >= c_io, u.T, 0.0)
-        if k + 1 < count:
-            rest = slice((k + 1) * n, m)
-            up = hi(v, w[s, rest], ((1,), (0,)))
-            w[rest, rest] = w[rest, rest] - hi(up, up, ((0,), (0,)))
-            low[rest, s] = up.T
-            low[s, rest] = jnp.zeros((n, m - (k + 1) * n), F32)
-            ups.append(up)
-        put(low.at[s], l_out.at[s], 1 + k)
-        acc = r_ref[s, :]
+        v, u = eliminate(block[k, k], n, buf)
+        factor[span(k), span(k)] = jnp.where(r_io >= c_io, u.T, 0.0)
+        for i in range(k + 1, count):
+            low[i, k] = full(block[i, k], v, NT)
+            factor[span(i), span(k)] = low[i, k]
+            factor[span(k), span(i)] = jnp.zeros((n, n), F32)
+            if i == k + 1:
+                block[i, i] = block[i, i] - full(low[i, k], low[i, k], NT)
+        for i in range(k + 2, count):
+            for j in range(k + 1, i + 1):
+                block[i, j] = block[i, j] - full(low[i, k], low[j, k], NT)
+        put(factor.at[span(k)], l_out.at[span(k)], 1 + k)
+        acc = r_ref[span(k), :]
         for j in range(k):
-            acc = acc - mm(ups[j][:, (k - j - 1) * n:(k - j) * n], xs[j], ((0,), (0,)))
-        x = mm(v, acc, ((1,), (0,)))
-        xs.append(x)
-        dirs[s, :] = x.astype(BF16)
-        put(dirs.at[s], d_out.at[s], 1 + count + k)
+            acc = acc - three(low[k, j], xs[j], NN)
+        xs.append(three(v, acc, NN))
+        dirs[span(k), :] = xs[k].astype(BF16)
+        put(dirs.at[span(k)], d_out.at[span(k)], 1 + count + k)
     for copy in pending:
         copy.wait()
 
@@ -336,8 +350,8 @@
         out_specs=(pl.BlockSpec(memory_space=pl.ANY),) * 3,
         scratch_shapes=[
             pltpu.VMEM((snaps, snaps), F32),
-            pltpu.VMEM((snaps, snaps), F32),
             pltpu.VMEM((snaps, own_points), BF16),
+            pltpu.VMEM((2, 9, 8, 2 * block), F32),
             dma((1 + 2 * (snaps // block),)),
         ],
         compiler_params=pltpu.CompilerParams(vmem_limit_bytes=32 << 20),

time: 77.2 us -> 74.9 us (0.970)
  Pallas kernels: 76.5 us -> 74.2 us
    pallas_call x1, Pallas kernels: 10.6 us -> 8.29 us  [shards(): pl.pallas_call(functools.partial(factor_kernel, block), out_shape=(jax.Sh...]
where the time goes in v5:
time: 74.9 us; the launch traced here: 74.8 us
  Pallas kernels  74.2 us (99%)
    pallas_call x1, Pallas kernels, shards(): pl.pallas_call(functools.partial(exchange, sides), out_shape=(jax.ShapeDt...  65.9 us
    pallas_call x1, Pallas kernels, shards(): pl.pallas_call(functools.partial(factor_kernel, block), out_shape=(jax.Sh...  8.29 us

profile of v5, /device:TPU:1, one launch (start us, length us, event | category | flops | bytes accessed | tf_op | source)
XLA Modules:
  0.0 74.8 jit_solution(13912898035125867834)
XLA Ops:
  0.6 65.9 %exchange.1 = (f32[256,256]{1,0:T(8,128)S(1)}, f32[256,256]{1,0:T(8,128)S(1)}, f32[256,1024]{1,0:T(8,128)S(1)}) custom-call(bf16[4096,256]{1,0:T(8,128)(2,1)} %b_hbm.1, bf16[256,4096]{1,0:T(8,128)(2,1)} %s_hbm.1), custom_call_target="tpu_custom_call" | custom-call | tf_op jit(solution)/shard_map/exchange/pallas_call | solution.py:302
  66.5 8.3 %factor.1 = (f32[256,256]{1,0:T(8,128)}, f32[256,256]{1,0:T(8,128)}, bf16[256,1024]{1,0:T(8,128)(2,1)}) custom-call(f32[256,256]{1,0:T(8,128)S(1)} %get-tuple-element.6.g_ref, f32[256,1024]{1,0:T(8,128)S(1)} %get-tuple-element.7.r_ref, f32[256,256]{1,0:T(8,128)S(1)} %get-tuple-element.8.c_ref), custom_call_target="tpu_custom_call" | custom-call | tf_op jit(solution)/shard_map/factor/pallas_call | solution.py:342

commit v6 on v5

--- a/solution.py
+++ b/solution.py
@@ -17,8 +17,8 @@
 SHARES = (7, 2, 4, 3)
 
 
-def exchange(sides, b_hbm, s_hbm, coef_o, gram_o, res_o, bv, sv, bfull, qfull, cbuf, pbuf, pbuf2, gbuf,
-             core_in, part, rs_in, ar_in, x_in, load_sem, bx_s, bx_r, core_s, core_r, rs_s, rs_r, ar_s, ar_r, x_s, x_r,
+def exchange(sides, b_hbm, s_hbm, coef_o, gram_o, res_o, bv, sv, bfull, qfull, cbuf, pbuf, psum,
+             p_core, p_rs, p_ar, gbuf, gsum, g_core, g_rs, g_ar, x_in, gall, load_sem, bx_s, bx_r, core_s, core_r, rs_s, rs_r, ar_s, ar_r, x_s, x_r,
              ag_s, ag_r, out_s, out_r, cag_s, cag_r, cout_s, cout_r):
     ny, nz, nx, points = sides
     row, x = lax.axis_index("rows"), lax.axis_index("cols")
@@ -95,38 +95,41 @@
                         preferred_element_type=F32)
         total = piece if total is None else total + piece
 
-    chunk = pl.ds(pl.multiple_of(one * rows, rows), rows)
     half = pl.ds(pl.multiple_of(c * HALF, HALF), HALF)
     other = pl.ds(pl.multiple_of((1 - c) * HALF, HALF), HALF)
 
     def half_chunk(t):
         return pl.ds(pl.multiple_of(c * HALF + t * rows, rows), rows)
 
-    def row_sum(phase, buf, value):
-        buf[...] = value
-        send(buf.at[other], core_in.at[phase], core_s.at[phase], core_r.at[phase], mate)
-        arrived(core_in.at[phase], core_r.at[phase])
-        part[phase] = buf[half, :] + core_in[phase]
+    def row_sum(phase, own_sum, buf, core_in, rs_in, ar_in):
+        send(buf.at[1 - c], core_in, core_s.at[phase], core_r.at[phase], mate)
+        arrived(core_in, core_r.at[phase])
+        own_sum[...] = buf[c] + core_in[...]
+        size = own_sum.shape[0] // ring
+
+        def piece(t):
+            return pl.ds(pl.multiple_of(t * size, size), size)
+
         for t in one_peers:
-            send(part.at[phase, pl.ds(pl.multiple_of(t * rows, rows), rows)], rs_in.at[phase, one],
-                 rs_s.at[phase, t], rs_r.at[phase, one], along_one(t))
-        rs_in[phase, one] = part[phase, chunk, :]
+            send(own_sum.at[piece(t)], rs_in.at[one], rs_s.at[phase, t], rs_r.at[phase, one], along_one(t))
+        rs_in[one] = own_sum[piece(one), :]
         for t in one_peers:
-            arrived(rs_in.at[phase, t], rs_r.at[phase, t])
-        got = rs_in[phase, 0]
+            arrived(rs_in.at[t], rs_r.at[phase, t])
+        got = rs_in[0]
         for i in range(1, ring):
-            got = got + rs_in[phase, i]
-        ar_in[phase, two] = got
+            got = got + rs_in[i]
+        ar_in[two] = got
         for t in two_peers:
-            send(ar_in.at[phase, two], ar_in.at[phase, two], ar_s.at[phase, t], ar_r.at[phase, two], along_two(t))
+            send(ar_in.at[two], ar_in.at[two], ar_s.at[phase, t], ar_r.at[phase, two], along_two(t))
         for t in two_peers:
-            arrived(ar_in.at[phase, t], ar_r.at[phase, t])
-        got = ar_in[phase, 0]
+            arrived(ar_in.at[t], ar_r.at[phase, t])
+        got = ar_in[0]
         for i in range(1, ring):
-            got = got + ar_in[phase, i]
+            got = got + ar_in[i]
         return got
 
-    own = row_sum(0, pbuf, total) * (math.sqrt(RANK) / points)
+    pbuf[0], pbuf[1] = total[:HALF], total[HALF:]
+    own = row_sum(0, psum, pbuf, p_core, p_rs, p_ar) * (math.sqrt(RANK) / points)
     mine = half_chunk(one)
     qfull[x, mine, :] = own.astype(BF16)
     for t in x_peers:
@@ -145,6 +148,14 @@
     send(qfull.at[:, half], qfull.at[:, half], out_s.at[0], out_r.at[0], mate)
     send_basis(3)
     arrived(qfull.at[:, other], out_r.at[0])
+
+    for t in one_peers:
+        arrived(cbuf.at[half_chunk(t)], cag_r.at[t])
+    send(cbuf.at[half], cbuf.at[half], cout_s, cout_r, mate)
+
+    def sent():
+        while pending:
+            pending.pop().wait_send()
 
     def from_modes(t):
         return lax.dot_general(qfull[t], bfull[t], (((1,), (1,)), ((), ())), preferred_element_type=F32)
@@ -160,31 +171,37 @@
     gram = lax.dot_general(residual, residual, (((1,), (1,)), ((), ())), precision=lax.Precision.HIGHEST,
                            preferred_element_type=F32) * (1.0 / points)
     res_o[...] = residual
-    for t in one_peers:
-        arrived(cbuf.at[half_chunk(t)], cag_r.at[t])
-    send(cbuf.at[half], cbuf.at[half], cout_s, cout_r, mate)
-    got = row_sum(1, pbuf2, gram)
+    q = HALF // 2
+    for h, (top, low) in enumerate(((0, 3 * q), (q, HALF))):
+        gbuf[h, :, :HALF] = gram[top:top + q, :HALF]
+        gbuf[h, :, HALF:] = gram[low:low + q, :]
+    got = row_sum(1, gsum, gbuf, g_core, g_rs, g_ar)
     x_in[x] = got
     for t in x_peers:
         send(x_in.at[x], x_in.at[x], x_s.at[1, t], x_r.at[1, x], along_x(t))
     arrived(cbuf.at[other], cout_r)
     coef_o[...] = cbuf[...].T
+    sent()
     for t in x_peers:
         arrived(x_in.at[t], x_r.at[1, t])
     got = x_in[0]
     for i in range(1, nx):
         got = got + x_in[i]
-    gbuf[mine, :] = got
-    for t in one_peers:
-        send(gbuf.at[mine], gbuf.at[mine], ag_s.at[1, t], ag_r.at[1, one], along_one(t))
-    for t in one_peers:
-        arrived(gbuf.at[half_chunk(t)], ag_r.at[1, t])
-    send(gbuf.at[half], gbuf.at[half], out_s.at[1], out_r.at[1], mate)
-    gram_o[half, :] = gbuf[half, :]
-    arrived(gbuf.at[other], out_r.at[1])
-    gram_o[other, :] = gbuf[other, :]
-    for copy in pending:
-        copy.wait_send()
+    size = q // ring
+
+    def gram_rows(t):
+        return gall.at[c, pl.ds(pl.multiple_of(t * size, size), size)]
+
+    gall[c, pl.ds(pl.multiple_of(one * size, size), size), :] = got
+    for t in one_peers:
+        send(gram_rows(one), gram_rows(one), ag_s.at[1, t], ag_r.at[1, one], along_one(t))
+    for t in one_peers:
+        arrived(gram_rows(t), ag_r.at[1, t])
+    send(gall.at[c], gall.at[c], out_s.at[1], out_r.at[1], mate)
+    gram_o[c] = gall[c]
+    sent()
+    arrived(gall.at[1 - c], out_r.at[1])
+    gram_o[1 - c] = gall[1 - c]
 
 
 def eliminate(a, n, buf):
@@ -252,7 +269,7 @@
 
 
 def factor_kernel(n, g_ref, r_ref, c_ref, c_out, l_out, d_out, factor, dirs, buf, sems):
-    count = g_ref.shape[0] // n
+    count = r_ref.shape[0] // n
     pending = []
 
     def put(src, dst, k):
@@ -266,7 +283,9 @@
     put(c_ref, c_out, 0)
     r_io = lax.broadcasted_iota(jnp.int32, (n, n), 0)
     c_io = lax.broadcasted_iota(jnp.int32, (n, n), 1)
-    block = {(i, k): g_ref[span(i), span(k)] for k in range(count) for i in range(k, count)}
+    place = ((0, 0), (1, 0), (1, HALF), (0, HALF))
+    block = {(i, k): g_ref[place[i][0], :, place[i][1] + k * n:place[i][1] + (k + 1) * n]
+             for k in range(count) for i in range(k, count)}
     low, xs = {}, []
     for k in range(count):
         v, u = eliminate(block[k, k], n, buf)
@@ -298,12 +317,17 @@
     snaps = snapshots.shape[0]
     n = max(ny, nz)
     dma = pltpu.SemaphoreType.DMA
-    chunk = HALF // n
+    packed = (2, HALF // 2, HALF + snaps)
+
+    def sum_buffers(rows, lanes):
+        shapes = [(2, rows, lanes), (rows, lanes), (rows, lanes), (n, rows // n, lanes), (n, rows // n, lanes)]
+        return [pltpu.VMEM(shape, F32) for shape in shapes]
+
     coefficients, gram, residual = pl.pallas_call(
         functools.partial(exchange, sides),
         out_shape=(
             jax.ShapeDtypeStruct((modes, snaps), F32),
-            jax.ShapeDtypeStruct((snaps, snaps), F32),
+            jax.ShapeDtypeStruct(packed, F32),
             jax.ShapeDtypeStruct((snaps, own_points), F32),
         ),
         in_specs=[pl.BlockSpec(memory_space=pltpu.HBM)] * 2,
@@ -314,14 +338,10 @@
             pltpu.VMEM((nx, own_points, modes), BF16),
             pltpu.VMEM((nx, snaps, modes), BF16),
             pltpu.VMEM((snaps, modes), F32),
-            pltpu.VMEM((snaps, modes), F32),
-            pltpu.VMEM((snaps, snaps), F32),
-            pltpu.VMEM((snaps, snaps), F32),
-            pltpu.VMEM((2, HALF, snaps), F32),
-            pltpu.VMEM((2, HALF, snaps), F32),
-            pltpu.VMEM((2, n, chunk, snaps), F32),
-            pltpu.VMEM((2, n, chunk, snaps), F32),
-            pltpu.VMEM((nx, chunk, snaps), F32),
+            *sum_buffers(HALF, modes),
+            *sum_buffers(*packed[1:]),
+            pltpu.VMEM((nx, packed[1] // n, packed[2]), F32),
+            pltpu.VMEM(packed, F32),
             dma((4,)),
             dma((len(SHARES), nx)), dma((len(SHARES), nx)),
             dma((2,)), dma((2,)),

time: 74.9 us -> 74.5 us (level)
  no operation moved by 1% of the time
where the time goes in v6:
time: 74.5 us; the launch traced here: 74.1 us
  Pallas kernels  73.5 us (99%)
    pallas_call x1, Pallas kernels, shards(): pl.pallas_call(functools.partial(exchange, sides), out_shape=(jax.ShapeDt...  65.2 us
    pallas_call x1, Pallas kernels, shards(): pl.pallas_call(functools.partial(factor_kernel, block), out_shape=(jax.Sh...  8.3 us

profile of v6, /device:TPU:1, one launch (start us, length us, event | category | flops | bytes accessed | tf_op | source)
XLA Modules:
  0.0 74.1 jit_solution(536221972156912005)
XLA Ops:
  0.6 65.2 %exchange.1 = (f32[256,256]{1,0:T(8,128)S(1)}, f32[2,64,384]{2,1,0:T(8,128)S(1)}, f32[256,1024]{1,0:T(8,128)S(1)}) custom-call(bf16[4096,256]{1,0:T(8,128)(2,1)} %b_hbm.1, bf16[256,4096]{1,0:T(8,128)(2,1)} %s_hbm.1), custom_call_target="tpu_custom_call" | custom-call | tf_op jit(solution)/shard_map/exchange/pallas_call | solution.py:326
  65.8 8.3 %factor.1 = (f32[256,256]{1,0:T(8,128)}, f32[256,256]{1,0:T(8,128)}, bf16[256,1024]{1,0:T(8,128)(2,1)}) custom-call(f32[2,64,384]{2,1,0:T(8,128)S(1)} %get-tuple-element.6.g_ref, f32[256,1024]{1,0:T(8,128)S(1)} %get-tuple-element.7.r_ref, f32[256,256]{1,0:T(8,128)S(1)} %get-tuple-element.8.c_ref), custom_call_target="tpu_custom_call" | custom-call | tf_op jit(solution)/shard_map/factor/pallas_call | solution.py:362

commit v7 on v6

--- a/solution.py
+++ b/solution.py
@@ -14,7 +14,7 @@
 F32 = jnp.float32
 BF16 = jnp.bfloat16
 HALF = 128
-SHARES = (7, 2, 4, 3)
+SHARES = (8, 2, 4, 2)
 
 
 def exchange(sides, b_hbm, s_hbm, coef_o, gram_o, res_o, bv, sv, bfull, qfull, cbuf, pbuf, psum,
@@ -157,20 +157,22 @@
         while pending:
             pending.pop().wait_send()
 
-    def from_modes(t):
-        return lax.dot_general(qfull[t], bfull[t], (((1,), (1,)), ((), ())), preferred_element_type=F32)
-
     load_own.wait()
-    recon = from_modes(x)
-    for t in reversed(x_peers):
-        for k, (start, size) in enumerate(spans):
+    gram = None
+    for k, (start, size) in enumerate(spans):
+        recon = None
+        for t in x_peers:
             arrived(bfull.at[t, pl.ds(start, size)], bx_r.at[k, t])
-        recon = recon + from_modes(t)
-    own_snaps = sv[:, pl.ds(pl.multiple_of(x * own_points, own_points), own_points)].astype(F32)
-    residual = own_snaps - recon * (1.0 / math.sqrt(RANK))
-    gram = lax.dot_general(residual, residual, (((1,), (1,)), ((), ())), precision=lax.Precision.HIGHEST,
-                           preferred_element_type=F32) * (1.0 / points)
-    res_o[...] = residual
+        for t in range(nx):
+            piece = lax.dot_general(qfull[t], bfull[t, start:start + size, :], (((1,), (1,)), ((), ())),
+                                    preferred_element_type=F32)
+            recon = piece if recon is None else recon + piece
+        snaps = sv[:, pl.ds(pl.multiple_of(x * own_points + start, math.gcd(start, size)), size)].astype(F32)
+        residual = snaps - recon * (1.0 / math.sqrt(RANK))
+        res_o[:, start:start + size] = residual
+        piece = full(residual, residual, NT)
+        gram = piece if gram is None else gram + piece
+    gram = gram * (1.0 / points)
     q = HALF // 2
     for h, (top, low) in enumerate(((0, 3 * q), (q, HALF))):
         gbuf[h, :, :HALF] = gram[top:top + q, :HALF]

time: 74.5 us -> 72.5 us (0.973)
  Pallas kernels: 73.5 us -> 71.8 us
    pallas_call x1, Pallas kernels: 65.2 us -> 63.5 us  [shards(): pl.pallas_call(functools.partial(exchange, sides), out_shape=(jax.ShapeDt...]
where the time goes in v7:
time: 72.5 us; the launch traced here: 72.4 us
  Pallas kernels  71.8 us (99%)
    pallas_call x1, Pallas kernels, shards(): pl.pallas_call(functools.partial(exchange, sides), out_shape=(jax.ShapeDt...  63.5 us
    pallas_call x1, Pallas kernels, shards(): pl.pallas_call(functools.partial(factor_kernel, block), out_shape=(jax.Sh...  8.29 us

profile of v7, /device:TPU:1, one launch (start us, length us, event | category | flops | bytes accessed | tf_op | source)
XLA Modules:
  0.0 72.4 jit_solution(12568981311272895970)
XLA Ops:
  0.6 63.5 %exchange.1 = (f32[256,256]{1,0:T(8,128)S(1)}, f32[2,64,384]{2,1,0:T(8,128)S(1)}, f32[256,1024]{1,0:T(8,128)S(1)}) custom-call(bf16[4096,256]{1,0:T(8,128)(2,1)} %b_hbm.1, bf16[256,4096]{1,0:T(8,128)(2,1)} %s_hbm.1), custom_call_target="tpu_custom_call" | custom-call | tf_op jit(solution)/shard_map/exchange/pallas_call | solution.py:328
  64.1 8.3 %factor.1 = (f32[256,256]{1,0:T(8,128)}, f32[256,256]{1,0:T(8,128)}, bf16[256,1024]{1,0:T(8,128)(2,1)}) custom-call(f32[2,64,384]{2,1,0:T(8,128)S(1)} %get-tuple-element.6.g_ref, f32[256,1024]{1,0:T(8,128)S(1)} %get-tuple-element.7.r_ref, f32[256,256]{1,0:T(8,128)S(1)} %get-tuple-element.8.c_ref), custom_call_target="tpu_custom_call" | custom-call | tf_op jit(solution)/shard_map/factor/pallas_call | solution.py:364
